TPU v7x, 32 devices: a whole 2x2x4 slice. The times are simulated.
32 devices in a mesh: tp: 2 (over x), wide: 16 (over z, y, core).
Axes of the slice: x: 2, y: 2, z: 4, core: 2. Of those that a mesh axis runs over, the one named last changes fastest.
Arguments:
- token_keys: bfloat16 [2048, 28672], P('tp', 'wide'), may hold values from -6 to 6
- resid_grad: bfloat16 [2048, 8192], P('wide', 'tp'), may hold values from -6 to 6
- kv_grad: bfloat16 [2048, 2048], P('wide', 'tp'), may hold values from -6 to 6
- kv_weight: bfloat16 [8192, 2048], P('wide', 'tp'), may hold values from -0.125 to 0.125
- editor_in: bfloat16 [8192, 1920], P('tp'), may hold values from -0.0625 to 0.0625
- editor_bias: float32 [1920], replicated, may hold values from -3 to 3
- editor_gain: float32 [8192], P('tp'), may hold values from 0.5 to 1.5
- editor_out: bfloat16 [1920, 8192], P(None, 'tp'), may hold values from -0.125 to 0.125
- prompt_len: int32 [32], replicated, may hold values from 1 to 63
Outputs:
- weight_update: bfloat16 [28672, 8192], P('wide', 'tp')
All inputs are finite; a program needn't handle non-finite values.
Results may differ from a plain program's by a relative error of at most 0.0055.
Values may be sent and summed in bfloat16 or wider, within the bound.
A program may use at most 128 MiB of HBM per device.

v0:
```python
import jax
import jax.numpy as jnp
from jax import lax
from jax.sharding import PartitionSpec as P

LEN = 64


EPSILON = 1e-06


def per_device(
    token_keys,
    resid_grad,
    kv_grad,
    kv_weight,
    editor_in,
    editor_bias,
    editor_gain,
    editor_out,
    prompt_len,
):
    own_rows = resid_grad.shape[0]
    local_width = resid_grad.shape[1]
    col_start = lax.axis_index("tp") * local_width
    partial_sum = lax.dot_general(
        kv_grad,
        lax.all_gather(kv_weight, "wide", axis=0, tiled=True),
        (((1,), (1,)), ((), ())),
        preferred_element_type=jnp.float32,
    )
    resid_float = resid_grad.astype(jnp.float32)
    own_cols = lax.dynamic_slice_in_dim(partial_sum, col_start, local_width, 1) + resid_float
    partial_sum = lax.dynamic_update_slice_in_dim(partial_sum, own_cols, col_start, 1)
    complete = lax.psum(partial_sum, "tp")
    gradient = lax.dynamic_slice_in_dim(complete, col_start, local_width, 1)
    squares = jnp.sum(complete * complete, axis=1, keepdims=True)
    scaled = (gradient * editor_gain).astype(jnp.bfloat16)
    hidden_part = jnp.dot(scaled, editor_in, preferred_element_type=jnp.float32)
    projected = lax.psum(hidden_part, "tp")
    full_width = local_width * lax.axis_size("tp")
    inv_rms = lax.rsqrt(squares / full_width + EPSILON)
    hidden = jnp.maximum(projected * inv_rms + editor_bias, 0.0).astype(jnp.bfloat16)
    local_examples = own_rows // LEN
    owner_starts = lax.dynamic_slice_in_dim(
        prompt_len, lax.axis_index("wide") * local_examples, local_examples, 0
    )
    starts = jnp.repeat(owner_starts, LEN, total_repeat_length=own_rows)
    position = jnp.arange(own_rows, dtype=jnp.int32) % LEN
    keep_mask = (position >= starts).astype(jnp.float32)
    edited = (
        (gradient + jnp.dot(hidden, editor_out, preferred_element_type=jnp.float32))
        * keep_mask[:, None]
    ).astype(jnp.bfloat16)
    edit_count = jnp.sum(LEN - prompt_len).astype(jnp.float32)
    key_table = lax.all_gather(token_keys, "tp", axis=0, tiled=True)
    initial = jnp.zeros((key_table.shape[1], local_width), jnp.float32)
    piece = lax.all_gather(edited, "wide", axis=0, tiled=True)
    key_block = lax.slice_in_dim(key_table, 0, piece.shape[0], axis=0)
    summed = initial + lax.dot_general(
        key_block, piece, (((0,), (0,)), ((), ())), preferred_element_type=jnp.float32
    )
    return (summed * lax.rsqrt(edit_count)).astype(jnp.bfloat16)


def solution(mesh):
    in_specs = (
        P("tp", "wide"),
        P("wide", "tp"),
        P("wide", "tp"),
        P("wide", "tp"),
        P("tp", None),
        P(),
        P("tp"),
        P(None, "tp"),
        P(),
    )
    out_specs = P("wide", "tp")
    return jax.shard_map(
        per_device, mesh=mesh, in_specs=in_specs, out_specs=out_specs, check_vma=False
    )
```

profile of v0, /device:TPU:1, one launch (start us, length us, event | category | flops | bytes accessed | tf_op | source)
XLA Modules:
  0.0 597.1 jit_solution(3047865533867975939)
XLA Ops:
  6.5 0.0 copy-start
  6.5 0.0 all-gather.4.cloned.1.call-start
  6.5 0.7 all-gather.4.cloned.1.call-update
  7.3 0.0 all-reduce.3.cloned.1.call-start
  7.3 0.0 copy-start.2
  7.3 131.6 %all-gather.4.cloned.1.call-done = bf16[8192,1024]{1,0:T(8,128)(2,1)} async-done(((bf16[512,1024]{1,0:T(8,128)(2,1)}), bf16[8192,1024]{1,0:T(8,128)(2,1)}) %all-gather.4.cloned.1.call-update) | async-done | bytes 16777232 | tf_op jit(solution)/shard_map/all_gather | solution.py:28
  139.0 13.3 %fusion.11 = f32[128,8192]{1,0:T(8,128)} fusion(bf16[128,1024]{1,0:T(8,128)(2,1)S(1)} %copy-done, bf16[8192,1024]{1,0:T(8,128)(2,1)} %all-gather.4.cloned.1.call-done), kind=kOutput, calls=%fused_computation.21 | convolution fusion | flops 2147483648 | bytes 21233664 | tf_op jit(solution)/shard_map/dot_general | solution.py:26
  152.3 0.0 copy-done.2
  152.3 3.1 add_dynamic-update-slice_fusion
  155.4 0.0 all-reduce.3.cloned.1.call-update
  155.5 0.0 copy-start.6
  155.5 0.0 copy-start.5
  155.5 0.0 all-reduce.5.cloned.1.call-start
  155.5 105.7 %all-reduce.3.cloned.1.call-done = f32[128,8192]{1,0:T(8,128)} async-done(((f32[128,8192]{1,0:T(8,128)}), f32[128,8192]{1,0:T(8,128)}) %all-reduce.3.cloned.1.call-update) | async-done | bytes 4194320 | tf_op jit(solution)/shard_map/psum | solution.py:35
  261.2 9.4 %fusion.3 = f32[128,1920]{1,0:T(8,128)} fusion(bf16[4096,1920]{1,0:T(8,128)(2,1)} %param.15, f32[128,8192]{1,0:T(8,128)} %all-reduce.3.cloned.1.call-done, s32[]{:T(128)S(6)} %select_n.31, f32[4096]{0:T(1024)S(1)} %copy-done.3), kind=kOutput, calls=%fused_computation.8 | convolution fusion | flops 2014314496 | bytes 18825220 | tf_op jit(solution)/shard_map/dot_general | solution.py:39
  270.6 0.0 all-reduce.5.cloned.1.call-update
  270.7 0.0 all-gather.8.cloned.1.call-start
  270.7 0.5 all-gather.8.cloned.1.call-update
  271.2 0.2 all-gather.6.cloned.1.call-start
  271.5 0.0 copy-done.6
  271.5 0.1 dynamic_slice.11
  271.6 0.6 fusion.10
  272.2 1.3 compare_convert_fusion
  273.4 2.5 multiply_reduce_fusion
  276.0 33.4 %all-reduce.5.cloned.1.call-done = f32[128,1920]{1,0:T(8,128)} async-done(((f32[128,1920]{1,0:T(8,128)}), f32[128,1920]{1,0:T(8,128)}) %all-reduce.5.cloned.1.call-update) | async-done | bytes 983056 | tf_op jit(solution)/shard_map/psum | solution.py:40
  309.4 9.8 %fusion.2 = bf16[128,4096]{1,0:T(8,128)(2,1)} fusion(bf16[1920,4096]{1,0:T(8,128)(2,1)} %param.18, f32[128,8192]{1,0:T(8,128)} %all-reduce.3.cloned.1.call-done, s32[]{:T(128)S(6)} %select_n.31, f32[128]{0:T(128)S(1)} %compare_convert_fusion, f32[128,1920]{1,0:T(8,128)} %all-reduce.5.cloned.1.call-done, f32[1920]{0:T(1024)S(1)} %copy-done.4, ...), kind=kOutput, calls=%fused_computation.4 | convolution fusion | flops 2015821824 | bytes 19866116 | tf_op jit(solution)/shard_map/dot_general | solution.py:52
  319.2 0.0 all-gather.6.cloned.1.call-update
  319.3 0.7 subtract_reduce_fusion
  320.6 82.5 %all-gather.8.cloned.1.call-done = bf16[2048,1792]{1,0:T(8,128)(2,1)} async-done(((bf16[1024,1792]{1,0:T(8,128)(2,1)}), bf16[2048,1792]{1,0:T(8,128)(2,1)}) %all-gather.8.cloned.1.call-update) | async-done | bytes 7340048 | tf_op jit(solution)/shard_map/all_gather | solution.py:56
  403.1 129.4 %all-gather.6.cloned.1.call-done = bf16[2048,4096]{1,0:T(8,128)(2,1)} async-done(((bf16[128,4096]{1,0:T(8,128)(2,1)}), bf16[2048,4096]{1,0:T(8,128)(2,1)}) %all-gather.6.cloned.1.call-update) | async-done | bytes 16777232 | tf_op jit(solution)/shard_map/all_gather | solution.py:58
  532.4 38.0 %fusion = bf16[1792,4096]{0,1:T(8,128)(2,1)} fusion(f32[]{:T(128)S(6)} %rsqrt.12, bf16[2048,4096]{1,0:T(8,128)(2,1)} %all-gather.6.cloned.1.call-done, bf16[2048,1792]{1,0:T(8,128)(2,1)} %all-gather.8.cloned.1.call-done), kind=kOutput, calls=%fused_computation.1 | convolution fusion | flops 30079451136 | bytes 38797316 | tf_op jit(solution)/shard_map/dot_general | solution.py:60
  570.4 20.1 %copy.10 = bf16[1792,4096]{1,0:T(8,128)(2,1)} copy(bf16[1792,4096]{0,1:T(8,128)(2,1)} %fusion) | data formatting | bytes 29360128 | tf_op jit(solution)/shard_map/convert_element_type | solution.py:63
  (9 shorter events, 0.0 us)
Async XLA Ops:
  6.5 132.4 %copy-start = (bf16[128,1024]{1,0:T(8,128)(2,1)S(1)}, bf16[128,1024]{1,0:T(8,128)(2,1)}, u32[]{:S(2)}) copy-start(bf16[128,1024]{1,0:T(8,128)(2,1)} %param.13) | copy-start | bytes 786436
  6.5 132.4 %all-gather.4.cloned.1.call-start = ((), (), s32[]{:S(2)}) async-start(), calls=%async_computation | async-start | bytes 17825792 | tf_op jit(solution)/shard_map/all_gather | solution.py:28
  7.3 254.0 %all-reduce.3.cloned.1.call-start = ((), (), s32[]{:S(2)}) async-start(), calls=%async_computation.1 | async-start | bytes 8388608 | tf_op jit(solution)/shard_map/psum | solution.py:35
  7.3 145.0 %copy-start.2 = (bf16[128,4096]{1,0:T(8,128)(2,1)S(1)}, bf16[128,4096]{1,0:T(8,128)(2,1)}, u32[]{:S(2)}) copy-start(bf16[128,4096]{1,0:T(8,128)(2,1)} %param.12) | copy-start | bytes 3145732
  152.3 108.9 %copy-start.3 = (f32[4096]{0:T(1024)S(1)}, f32[4096]{0:T(1024)}, u32[]{:S(2)}) copy-start(f32[4096]{0:T(1024)} %param.17) | copy-start | bytes 49156
  155.5 116.0 %copy-start.6 = (s32[32]{0:T(128)S(1)}, s32[32]{0:T(128)}, u32[]{:S(2)}) copy-start(s32[32]{0:T(128)} %param.19) | copy-start | bytes 388
  155.5 116.7 %copy-start.5 = (pred[128]{0:T(512)(128)(4,1)S(1)}, pred[128]{0:T(512)(128)(4,1)}, u32[]{:S(2)}) copy-start(pred[128]{0:T(512)(128)(4,1)} %constant.122) | copy-start | bytes 388
  155.5 154.0 %all-reduce.5.cloned.1.call-start = ((), (), s32[]{:S(2)}) async-start(), calls=%async_computation.2 | async-start | bytes 1966080 | tf_op jit(solution)/shard_map/psum | solution.py:40
  270.6 38.8 %copy-start.4 = (f32[1920]{0:T(1024)S(1)}, f32[1920]{0:T(1024)}, u32[]{:S(2)}) copy-start(f32[1920]{0:T(1024)} %param.16) | copy-start | bytes 23044
  270.7 132.4 %all-gather.8.cloned.1.call-start = ((), (), s32[]{:S(2)}) async-start(), calls=%async_computation.4 | async-start | bytes 11010048 | tf_op jit(solution)/shard_map/all_gather | solution.py:56
  271.2 261.2 %all-gather.6.cloned.1.call-start = ((), (), s32[]{:S(2)}) async-start(), calls=%async_computation.3 | async-start | bytes 17825792 | tf_op jit(solution)/shard_map/all_gather | solution.py:58
  570.4 20.1 %copy-start.1 = (bf16[128,1024]{1,0:T(8,128)(2,1)S(1)}, bf16[128,1024]{1,0:T(8,128)(2,1)}, u32[]{:S(2)}) copy-start(bf16[128,1024]{1,0:T(8,128)(2,1)} %param.13) | copy-start | bytes 786436
Sparse Core Ops, SparseCore 0:
  9.5 129.3 all-gather.3
  155.6 105.6 all-reduce.2
  270.8 38.6 all-reduce.4
  310.8 92.1 all-gather.7
  405.1 127.3 all-gather.5
where the time goes:
time: 598 us; the launch traced here: 597 us
  waiting for transfers between devices  484 us (81%)
  matrix products  70.5 us (12%)
  local copies, waits for them, and re-layouts  20.8 us (3%)
  between operations  13.9 us (2%)
  other arithmetic  7.61 us (1%)
    all_gather x1, waiting for transfers between devices, per_device(): lax.all_gather(kv_weight, 'wide', axis=0, tiled=True)  132 us
    all_gather x1, waiting for transfers between devices, per_device(): piece = lax.all_gather(edited, 'wide', axis=0, tiled=True)  129 us
    psum x1, waiting for transfers between devices, per_device(): complete = lax.psum(partial_sum, 'tp')  106 us
    all_gather x1, waiting for transfers between devices, per_device(): key_table = lax.all_gather(token_keys, 'tp', axis=0, tiled=True)  82.5 us
    dot_general x1, matrix products, per_device(): lax.dot_general(key_block, piece, (((0,), (0,)), ((), ())), preferred_ele...  38 us
    psum x1, waiting for transfers between devices, per_device(): projected = lax.psum(hidden_part, 'tp')  33.4 us
    convert_element_type x1, local copies, waits for them, and re-layouts, per_device(): return (summed * lax.rsqrt(edit_count)).astype(jnp.bfloat16)  20.1 us
    dot_general x1, matrix products, per_device(): lax.dot_general(kv_grad, lax.all_gather(kv_weight, 'wide', axis=0, tiled=...  13.3 us
  transfers between devices with their start and end apart: 5, of which 5 were waited for; matrix products, arithmetic and copies ran while one was open for 3% of the time, Pallas kernels for 0%

commit v1 on v0

v1 whole, which is shorter than its diff:
```python
import functools

import jax
import jax.numpy as jnp
from jax import lax
from jax.experimental import pallas as pl
from jax.experimental.pallas import tpu as pltpu
from jax.sharding import PartitionSpec as P

LEN = 64
EPSILON = 1e-06
MESH = pl.DeviceIdType.MESH
F32, BF16 = jnp.float32, jnp.bfloat16
MIB = 1 << 20


def gather_blocks(piece, chunks, outer, inner, sems, consume):
    line_send, peer_send, pair_send, recv = sems
    me = lax.axis_index("wide")
    a, b, c = me // (2 * inner), (me // 2) % inner, me % 2

    def ident(a1, b1, c1):
        return (a1 * inner + b1) * 2 + c1

    def copy(owner, q, send, target):
        ref = piece(owner, q)
        return pltpu.make_async_remote_copy(
            src_ref=ref, dst_ref=ref, send_sem=send, recv_sem=recv.at[owner, q],
            device_id={"wide": target}, device_id_type=MESH,
        )

    def arrived(owner, q):
        copy(owner, q, pair_send.at[owner, q], ident(a, b, 1 - c)).wait_recv()

    def line_copies(dist, sign, q, do):
        a1 = a + sign * dist
        owner = ident(a1, b, c)
        for way in (-1, 1):
            onward = a + way
            goes = (onward >= 0) & (onward < outer) & ((dist == 0) | (way == -sign))

            @pl.when(goes)
            def _():
                do(copy(owner, q, line_send.at[owner, q, (way + 1) // 2], ident(onward, b, c)))

        for k in range(1, inner):
            do(copy(owner, q, peer_send.at[owner, q, k - 1], ident(a, (b + k) % inner, c)))
        do(copy(owner, q, pair_send.at[owner, q], ident(a, b, 1 - c)))

    def on_line(i, todo):
        for sign in (-1, 1):
            dist, q = i // chunks, i % chunks
            a1 = a + sign * dist
            here = (i >= 0) & (dist < outer) & (a1 >= 0) & (a1 < outer)
            if sign == -1:
                here = here & (dist > 0)

            @pl.when(here)
            def _():
                todo(dist, sign, q, a1)

    def step(i, carry):
        def first(dist, sign, q, a1):
            owner = ident(a1, b, c)

            @pl.when(dist > 0)
            def _():
                arrived(owner, q)

            line_copies(dist, sign, q, lambda made: made.start())
            consume(owner, q)

        on_line(i, first)

        def second(dist, sign, q, a1):
            for k in range(1, inner):
                owner = ident(a1, (b + k) % inner, c)
                arrived(owner, q)
                copy(owner, q, pair_send.at[owner, q], ident(a, b, 1 - c)).start()
                consume(owner, q)

        on_line(i - chunks, second)

        def third(dist, sign, q, a1):
            for k in range(inner):
                owner = ident(a1, (b + k) % inner, 1 - c)
                arrived(owner, q)
                consume(owner, q)

        on_line(i - 2 * chunks, third)
        return carry

    lax.fori_loop(0, (outer + 2) * chunks, step, 0)

    def drain():
        def finish(i, carry):
            def sent(dist, sign, q, a1):
                line_copies(dist, sign, q, lambda made: made.wait_send())
                for k in range(1, inner):
                    owner = ident(a1, (b + k) % inner, c)
                    copy(owner, q, pair_send.at[owner, q], ident(a, b, 1 - c)).wait_send()

            on_line(i, sent)
            return carry

        lax.fori_loop(0, outer * chunks, finish, 0)

    return drain


def edit_kernel(
    tp, n, outer, inner, chunks, width,
    keys, resid, kv_grad, kv_weight, editor_in, bias, gain, editor_out, prompt_len,
    keys_all, edited_all,
    kv_all, product, parts, grad, in_held, out_held, hid, hid_send, hid_recv, sq_send, sq_recv, edited,
    local, line1, peer1, pair1, recv1, line2, peer2, pair2, recv2,
    part_send, part_recv, hid_ssem, hid_rsem, sq_ssem, sq_rsem, key_ssem, key_rsem,
):
    t, w = lax.axis_index("tp"), lax.axis_index("wide")
    rows = resid.shape[0]
    columns = resid.shape[1]
    tile = kv_weight.shape[0]
    per = columns // tile
    key_rows = keys.shape[0]
    owner_t, slot = w // per, w % per

    in_copy = pltpu.make_async_copy(editor_in, in_held, local.at[0])
    out_copy = pltpu.make_async_copy(editor_out, out_held, local.at[1])
    own_keys = pltpu.make_async_copy(keys, keys_all.at[pl.ds(t * key_rows, key_rows)], local.at[2])
    in_copy.start()
    out_copy.start()

    barrier = pltpu.get_barrier_semaphore()

    def greet(i, carry):
        @pl.when(i != t * n + w)
        def _():
            pl.semaphore_signal(barrier, inc=1, device_id={"tp": i // n, "wide": i % n}, device_id_type=MESH)

        return carry

    lax.fori_loop(0, tp * n, greet, 0)
    kv_all[w] = kv_grad[...]
    pl.semaphore_wait(barrier, tp * n - 1)

    def part_copy(owner):
        return pltpu.make_async_remote_copy(
            src_ref=product.at[owner], dst_ref=parts.at[t, slot],
            send_sem=part_send.at[owner], recv_sem=part_recv.at[t, slot],
            device_id={"tp": owner_t, "wide": owner}, device_id_type=MESH,
        )

    def multiply(owner, q):
        term = lax.dot_general(
            kv_all[owner], kv_weight[...], (((1,), (1,)), ((), ())), preferred_element_type=F32
        ).astype(BF16)
        stays = (owner_t == t) & (owner == w)

        @pl.when(stays)
        def _():
            parts[t, slot] = term

        @pl.when(jnp.logical_not(stays))
        def _():
            product[owner] = term
            part_copy(owner).start()

    drain1 = gather_blocks(
        lambda owner, q: kv_all.at[owner], 1, outer, inner, (line1, peer1, pair1, recv1), multiply
    )
    in_copy.wait()

    hid[...] = jnp.zeros_like(hid)
    sq_send[...] = jnp.zeros_like(sq_send)

    def take(k, carry):
        for source in range(tp):
            @pl.when(jnp.logical_not((source == t) & (t * per + k == w)))
            def _():
                pltpu.make_async_remote_copy(
                    src_ref=product.at[0], dst_ref=parts.at[source, k],
                    send_sem=part_send.at[0], recv_sem=part_recv.at[source, k],
                    device_id={"tp": t, "wide": w}, device_id_type=MESH,
                ).wait_recv()

        at = pl.ds(pl.multiple_of(k * tile, tile), tile)
        term = parts[0, k].astype(F32)
        for source in range(1, tp):
            term = term + parts[source, k].astype(F32)
        block = term + resid[:, at].astype(F32)
        grad[:, at] = block
        sq_send[...] += jnp.broadcast_to(jnp.sum(block * block, axis=1, keepdims=True), sq_send.shape)
        scaled = (block * gain[:, at]).astype(BF16)
        hid[...] += jnp.dot(scaled, in_held[at, :], preferred_element_type=F32)
        return carry

    lax.fori_loop(0, per, take, 0)
    hid_send[...] = hid[...].astype(BF16)

    def hid_copies(k):
        to = (t + k) % tp
        return (
            pltpu.make_async_remote_copy(
                src_ref=hid_send, dst_ref=hid_recv.at[k - 1], send_sem=hid_ssem.at[k - 1],
                recv_sem=hid_rsem.at[k - 1], device_id={"tp": to}, device_id_type=MESH),
            pltpu.make_async_remote_copy(
                src_ref=sq_send, dst_ref=sq_recv.at[k - 1], send_sem=sq_ssem.at[k - 1],
                recv_sem=sq_rsem.at[k - 1], device_id={"tp": to}, device_id_type=MESH),
        )

    def key_copy(k):
        return pltpu.make_async_remote_copy(
            src_ref=keys, dst_ref=keys_all.at[pl.ds(t * key_rows, key_rows)], send_sem=key_ssem.at[k - 1],
            recv_sem=key_rsem.at[k - 1], device_id={"tp": (t + k) % tp}, device_id_type=MESH)

    for k in range(1, tp):
        for made in hid_copies(k):
            made.start()
    own_keys.start()
    for k in range(1, tp):
        key_copy(k).start()
    out_copy.wait()
    squares = sq_send[:, :1]
    for k in range(1, tp):
        for made in hid_copies(k):
            made.wait_recv()
        hid[...] += hid_recv[k - 1].astype(F32)
        squares = squares + sq_recv[k - 1][:, :1]
    inv_rms = lax.rsqrt(squares / width + EPSILON)
    hid_send_free = [made for k in range(1, tp) for made in hid_copies(k)]
    for made in hid_send_free:
        made.wait_send()
    hid_send[...] = jnp.maximum(hid[...] * inv_rms + bias[...], 0.0).astype(BF16)

    examples = rows // LEN
    masks = []
    for e in range(examples):
        start = prompt_len[w * examples + e]
        masks.append((lax.broadcasted_iota(jnp.int32, (LEN, 1), 0) >= start).astype(F32))
    keep = jnp.concatenate(masks, axis=0)

    def edit(k, carry):
        at = pl.ds(pl.multiple_of(k * tile, tile), tile)
        total = grad[:, at] + jnp.dot(hid_send[...], out_held[:, at], preferred_element_type=F32)
        edited[:, at] = (total * keep).astype(BF16)
        return carry

    lax.fori_loop(0, per, edit, 0)
    own_edited = pltpu.make_async_copy(
        edited, edited_all.at[pl.ds(pl.multiple_of(w * rows, rows), rows)], local.at[3])
    own_edited.start()
    own_edited.wait()

    part = rows // chunks
    drain2 = gather_blocks(
        lambda owner, q: edited_all.at[pl.ds(pl.multiple_of(owner * rows + q * part, part), part)],
        chunks, outer, inner, (line2, peer2, pair2, recv2), lambda owner, q: None,
    )

    drain1()

    def sent(i, carry):
        @pl.when(jnp.logical_not((owner_t == t) & (i == w)))
        def _():
            part_copy(i).wait_send()

        return carry

    lax.fori_loop(0, n, sent, 0)
    drain2()
    own_keys.wait()
    for k in range(1, tp):
        key_copy(k).wait_send()
        source = (t + tp - k) % tp
        pltpu.make_async_remote_copy(
            src_ref=keys, dst_ref=keys_all.at[pl.ds(source * key_rows, key_rows)], send_sem=key_ssem.at[k - 1],
            recv_sem=key_rsem.at[k - 1], device_id={"tp": source}, device_id_type=MESH).wait_recv()


def update_kernel(prompt_len, keys, edited, out):
    def count(i, total):
        return total + (LEN - prompt_len[i])

    edit_count = lax.fori_loop(0, prompt_len.shape[0], count, 0)
    scale = lax.rsqrt(jnp.full((1, 1), edit_count, jnp.int32).astype(F32))
    summed = lax.dot_general(keys[...], edited[...], (((0,), (0,)), ((), ())), preferred_element_type=F32)
    out[...] = (summed * scale).astype(BF16)


def per_device(
    tp, n, token_keys, resid_grad, kv_grad, kv_weight, editor_in, editor_bias, editor_gain, editor_out, prompt_len
):
    outer = 4 if n % 8 == 0 else 1
    inner = n // (2 * outer)
    chunks = 2
    rows, columns = resid_grad.shape
    tile, kv_local = kv_weight.shape
    per = columns // tile
    rank = editor_in.shape[1]
    key_rows, key_columns = token_keys.shape
    vmem = pl.BlockSpec(memory_space=pltpu.VMEM)
    hbm = pl.BlockSpec(memory_space=pl.ANY)
    smem = pl.BlockSpec(memory_space=pltpu.SMEM)
    dma = pltpu.SemaphoreType.DMA
    peers = max(inner - 1, 1)
    others = max(tp - 1, 1)
    keys_all, edited_all = pl.pallas_call(
        functools.partial(edit_kernel, tp, n, outer, inner, chunks, columns * tp),
        out_shape=(
            jax.ShapeDtypeStruct((tp * key_rows, key_columns), BF16),
            jax.ShapeDtypeStruct((n * rows, columns), BF16),
        ),
        in_specs=[hbm, vmem, vmem, vmem, hbm, vmem, vmem, hbm, smem],
        out_specs=(hbm, hbm),
        scratch_shapes=[
            pltpu.VMEM((n, rows, kv_local), BF16),
            pltpu.VMEM((n, rows, tile), BF16),
            pltpu.VMEM((tp, per, rows, tile), BF16),
            pltpu.VMEM((rows, columns), F32),
            pltpu.VMEM(editor_in.shape, BF16),
            pltpu.VMEM(editor_out.shape, BF16),
            pltpu.VMEM((rows, rank), F32),
            pltpu.VMEM((rows, rank), BF16),
            pltpu.VMEM((others, rows, rank), BF16),
            pltpu.VMEM((rows, 128), F32),
            pltpu.VMEM((others, rows, 128), F32),
            pltpu.VMEM((rows, columns), BF16),
            dma((4,)),
            dma((n, 1, 2)), dma((n, 1, peers)), dma((n, 1)), dma((n, 1)),
            dma((n, chunks, 2)), dma((n, chunks, peers)), dma((n, chunks)), dma((n, chunks)),
            dma((n,)), dma((tp, per)),
            dma((others,)), dma((others,)), dma((others,)), dma((others,)), dma((others,)), dma((others,)),
        ],
        compiler_params=pltpu.CompilerParams(
            collective_id=0, has_side_effects=True, vmem_limit_bytes=60 * MIB
        ),
    )(
        token_keys, resid_grad, kv_grad, kv_weight, editor_in, editor_bias.reshape(1, -1),
        editor_gain.reshape(1, -1), editor_out, prompt_len,
    )
    block = min(columns, 512)
    tokens = keys_all.shape[0]
    return pl.pallas_call(
        update_kernel,
        grid=(columns // block,),
        out_shape=jax.ShapeDtypeStruct((key_columns, columns), BF16),
        in_specs=[
            smem,
            pl.BlockSpec((tokens, key_columns), lambda i: (0, 0)),
            pl.BlockSpec((tokens, block), lambda i: (0, i)),
        ],
        out_specs=pl.BlockSpec((key_columns, block), lambda i: (0, i)),
        compiler_params=pltpu.CompilerParams(vmem_limit_bytes=60 * MIB),
    )(prompt_len, keys_all, edited_all)


def solution(mesh):
    in_specs = (
        P("tp", "wide"),
        P("wide", "tp"),
        P("wide", "tp"),
        P("wide", "tp"),
        P("tp", None),
        P(),
        P("tp"),
        P(None, "tp"),
        P(),
    )
    out_specs = P("wide", "tp")
    return jax.shard_map(
        functools.partial(per_device, mesh.shape["tp"], mesh.shape["wide"]),
        mesh=mesh, in_specs=in_specs, out_specs=out_specs, check_vma=False,
    )
```

time: 598 us -> 245 us (0.41)
  waiting for transfers between devices: 484 us -> 0 us
  Pallas kernels: 0 us -> 243 us
  matrix products: 70.5 us -> 0 us
  local copies, waits for them, and re-layouts: 20.8 us -> 1.3 us
  between operations: 13.9 us -> 0.01 us
  other arithmetic: 7.61 us -> 0 us
    all_gather x3 -> x0, waiting for transfers between devices: 343 us -> none  [the longest x1 132 us: per_device(): lax.all_gather(kv_weight, 'wide', axis=0, tiled=True)]
    pallas_call x0 -> x2, Pallas kernels: none -> 243 us  [the longest x1 204 us: per_device(): pl.pallas_call(functools.partial(edit_kernel, tp, n, outer, inner, chunks...]
    psum x2 -> x0, waiting for transfers between devices: 139 us -> none  [the longest x1 106 us: per_device(): complete = lax.psum(partial_sum, 'tp')]
    dot_general x4 -> x0, matrix products: 70.5 us -> none  [the longest x1 38 us: per_device(): lax.dot_general(key_block, piece, (((0,), (0,)), ((), ())), preferred_ele...]
    convert_element_type x1 -> x0, local copies, waits for them, and re-layouts: 20.1 us -> none  [per_device(): return (summed * lax.rsqrt(edit_count)).astype(jnp.bfloat16)]
  transfers between devices with their start and end apart: 5 -> 0, of which waited for: 5 -> 0; matrix products, arithmetic and copies ran while one was open for 3% -> 0% of each run, Pallas kernels for 0% -> 0%
where the time goes in v1:
time: 245 us; the launch traced here: 244 us
  Pallas kernels  243 us (99%)
    pallas_call x1, Pallas kernels, per_device(): pl.pallas_call(functools.partial(edit_kernel, tp, n, outer, inner, chunks...  204 us
    pallas_call x1, Pallas kernels, per_device(): pl.pallas_call(update_kernel, grid=(columns // block,), out_shape=jax.Sha...  38.6 us

profile of v1, /device:TPU:1, one launch (start us, length us, event | category | flops | bytes accessed | tf_op | source)
XLA Modules:
  0.0 244.3 jit_solution(14215700965008591455)
XLA Ops:
  0.0 1.3 reshape.6.bias
  1.3 204.4 %shard_map.91 = (bf16[2048,1792]{1,0:T(8,128)(2,1)}, bf16[2048,4096]{1,0:T(8,128)(2,1)}) custom-call(bf16[1024,1792]{1,0:T(8,128)(2,1)} %keys.1, bf16[128,4096]{1,0:T(8,128)(2,1)} %resid.1, bf16[128,1024]{1,0:T(8,128)(2,1)} %kv_grad.1, bf16[512,1024]{1,0:T(8,128)(2,1)} %kv_weight.1, bf16[4096,1920]{1,0:T(8,128)(2,1)} %editor_in.1, f32[1,1920]{1,0:T(1,128)} %reshape.6.bias, ...), custom_call_target="tpu_custom_call" | custom-call | tf_op jit(solution)/shard_map/pallas_call | solution.py:307
  205.7 38.6 %shard_map.92 = bf16[1792,4096]{1,0:T(8,128)(2,1)} custom-call(s32[32]{0:T(128)} %prompt_len.3, bf16[2048,1792]{1,0:T(8,128)(2,1)} %get-tuple-element.7.keys, bf16[2048,4096]{1,0:T(8,128)(2,1)} %get-tuple-element.8.edited), custom_call_target="tpu_custom_call" | custom-call | tf_op jit(solution)/shard_map/pallas_call | solution.py:343

commit v2 on v1

--- a/solution.py
+++ b/solution.py
@@ -112,7 +112,7 @@
     tp, n, outer, inner, chunks, width,
     keys, resid, kv_grad, kv_weight, editor_in, bias, gain, editor_out, prompt_len,
     keys_all, edited_all,
-    kv_all, product, parts, grad, in_held, out_held, hid, hid_send, hid_recv, sq_send, sq_recv, edited,
+    kv_all, product, parts, grad, in_held, out_held, hid, hid_send, hid_recv, sq_send, sq_recv, edited, kv_turned,
     local, line1, peer1, pair1, recv1, line2, peer2, pair2, recv2,
     part_send, part_recv, hid_ssem, hid_rsem, sq_ssem, sq_rsem, key_ssem, key_rsem,
 ):
@@ -129,6 +129,7 @@
     own_keys = pltpu.make_async_copy(keys, keys_all.at[pl.ds(t * key_rows, key_rows)], local.at[2])
     in_copy.start()
     out_copy.start()
+    own_keys.start()
 
     barrier = pltpu.get_barrier_semaphore()
 
@@ -141,6 +142,7 @@
 
     lax.fori_loop(0, tp * n, greet, 0)
     kv_all[w] = kv_grad[...]
+    kv_turned[...] = kv_weight[...].T
     pl.semaphore_wait(barrier, tp * n - 1)
 
     def part_copy(owner):
@@ -152,7 +154,7 @@
 
     def multiply(owner, q):
         term = lax.dot_general(
-            kv_all[owner], kv_weight[...], (((1,), (1,)), ((), ())), preferred_element_type=F32
+            kv_all[owner], kv_turned[...], (((1,), (0,)), ((), ())), preferred_element_type=F32
         ).astype(BF16)
         stays = (owner_t == t) & (owner == w)
 
@@ -216,7 +218,6 @@
     for k in range(1, tp):
         for made in hid_copies(k):
             made.start()
-    own_keys.start()
     for k in range(1, tp):
         key_copy(k).start()
     out_copy.wait()
@@ -325,6 +326,7 @@
             pltpu.VMEM((rows, 128), F32),
             pltpu.VMEM((others, rows, 128), F32),
             pltpu.VMEM((rows, columns), BF16),
+            pltpu.VMEM((kv_local, tile), BF16),
             dma((4,)),
             dma((n, 1, 2)), dma((n, 1, peers)), dma((n, 1)), dma((n, 1)),
             dma((n, chunks, 2)), dma((n, chunks, peers)), dma((n, chunks)), dma((n, chunks)),
@@ -338,7 +340,7 @@
         token_keys, resid_grad, kv_grad, kv_weight, editor_in, editor_bias.reshape(1, -1),
         editor_gain.reshape(1, -1), editor_out, prompt_len,
     )
-    block = min(columns, 512)
+    block = min(columns, 1024)
     tokens = keys_all.shape[0]
     return pl.pallas_call(
         update_kernel,

time: 245 us -> 244 us (level)
  no operation moved by 1% of the time
where the time goes in v2:
time: 244 us
  Pallas kernels  243 us (100%)
    pallas_call x1, Pallas kernels, per_device(): pl.pallas_call(functools.partial(edit_kernel, tp, n, outer, inner, chunks...  204 us
    pallas_call x1, Pallas kernels, per_device(): pl.pallas_call(update_kernel, grid=(columns // block,), out_shape=jax.Sha...  38.2 us

profile of v2, /device:TPU:1, one launch (start us, length us, event | category | flops | bytes accessed | tf_op | source)
XLA Modules:
  0.0 243.8 jit_solution(13683896440400768109)
XLA Ops:
  0.0 1.3 reshape.6.bias
  1.3 204.3 %shard_map.91 = (bf16[2048,1792]{1,0:T(8,128)(2,1)}, bf16[2048,4096]{1,0:T(8,128)(2,1)}) custom-call(bf16[1024,1792]{1,0:T(8,128)(2,1)} %keys.1, bf16[128,4096]{1,0:T(8,128)(2,1)} %resid.1, bf16[128,1024]{1,0:T(8,128)(2,1)} %kv_grad.1, bf16[512,1024]{1,0:T(8,128)(2,1)} %kv_weight.1, bf16[4096,1920]{1,0:T(8,128)(2,1)} %editor_in.1, f32[1,1920]{1,0:T(1,128)} %reshape.6.bias, ...), custom_call_target="tpu_custom_call" | custom-call | tf_op jit(solution)/shard_map/pallas_call | solution.py:308
  205.6 38.2 %shard_map.92 = bf16[1792,4096]{1,0:T(8,128)(2,1)} custom-call(s32[32]{0:T(128)} %prompt_len.3, bf16[2048,1792]{1,0:T(8,128)(2,1)} %get-tuple-element.7.keys, bf16[2048,4096]{1,0:T(8,128)(2,1)} %get-tuple-element.8.edited), custom_call_target="tpu_custom_call" | custom-call | tf_op jit(solution)/shard_map/pallas_call | solution.py:345

commit v3 on v2

--- a/solution.py
+++ b/solution.py
@@ -168,7 +168,9 @@
             part_copy(owner).start()
 
     drain1 = gather_blocks(
-        lambda owner, q: kv_all.at[owner], 1, outer, inner, (line1, peer1, pair1, recv1), multiply
+        lambda owner, q: kv_all.at[owner, pl.ds(pl.multiple_of(q * (rows // chunks), rows // chunks), rows // chunks)],
+        chunks, outer, inner, (line1, peer1, pair1, recv1),
+        lambda owner, q: pl.when(q == chunks - 1)(lambda: multiply(owner, q)),
     )
     in_copy.wait()
 
@@ -328,7 +330,7 @@
             pltpu.VMEM((rows, columns), BF16),
             pltpu.VMEM((kv_local, tile), BF16),
             dma((4,)),
-            dma((n, 1, 2)), dma((n, 1, peers)), dma((n, 1)), dma((n, 1)),
+            dma((n, chunks, 2)), dma((n, chunks, peers)), dma((n, chunks)), dma((n, chunks)),
             dma((n, chunks, 2)), dma((n, chunks, peers)), dma((n, chunks)), dma((n, chunks)),
             dma((n,)), dma((tp, per)),
             dma((others,)), dma((others,)), dma((others,)), dma((others,)), dma((others,)), dma((others,)),

time: 244 us -> 244 us (level)
  no operation moved by 1% of the time
where the time goes in v3:
time: 244 us
  Pallas kernels  243 us (100%)
    pallas_call x1, Pallas kernels, per_device(): pl.pallas_call(functools.partial(edit_kernel, tp, n, outer, inner, chunks...  205 us
    pallas_call x1, Pallas kernels, per_device(): pl.pallas_call(update_kernel, grid=(columns // block,), out_shape=jax.Sha...  38.3 us

profile of v3, /device:TPU:1, one launch (start us, length us, event | category | flops | bytes accessed | tf_op | source)
XLA Modules:
  0.0 244.1 jit_solution(7108921688919627136)
XLA Ops:
  0.0 1.3 reshape.6.bias
  1.3 204.5 %shard_map.91 = (bf16[2048,1792]{1,0:T(8,128)(2,1)}, bf16[2048,4096]{1,0:T(8,128)(2,1)}) custom-call(bf16[1024,1792]{1,0:T(8,128)(2,1)} %keys.1, bf16[128,4096]{1,0:T(8,128)(2,1)} %resid.1, bf16[128,1024]{1,0:T(8,128)(2,1)} %kv_grad.1, bf16[512,1024]{1,0:T(8,128)(2,1)} %kv_weight.1, bf16[4096,1920]{1,0:T(8,128)(2,1)} %editor_in.1, f32[1,1920]{1,0:T(1,128)} %reshape.6.bias, ...), custom_call_target="tpu_custom_call" | custom-call | tf_op jit(solution)/shard_map/pallas_call | solution.py:310
  205.8 38.3 %shard_map.92 = bf16[1792,4096]{1,0:T(8,128)(2,1)} custom-call(s32[32]{0:T(128)} %prompt_len.3, bf16[2048,1792]{1,0:T(8,128)(2,1)} %get-tuple-element.7.keys, bf16[2048,4096]{1,0:T(8,128)(2,1)} %get-tuple-element.8.edited), custom_call_target="tpu_custom_call" | custom-call | tf_op jit(solution)/shard_map/pallas_call | solution.py:347
